TPU v7x, 32 devices: a whole 2x2x4 slice. The times are simulated.
32 devices in a mesh: seq: 8 (over z, y), head: 4 (over x, core).
Axes of the slice: x: 2, y: 2, z: 4, core: 2. Of those that a mesh axis runs over, the one named last changes fastest.
Arguments:
- queries: bfloat16 [2048, 16, 128], P('seq', 'head'), may hold values from -42 to 42, as said below
- keys: bfloat16 [2048, 4, 128], P('seq', 'head'), may hold values from -6 to 6
- values: bfloat16 [2048, 4, 128], P('seq', 'head'), may hold values from -6 to 6
- feat_q: bfloat16 [16, 128, 128], P('head'), may hold values from -0.5 to 0.5
- feat_k: bfloat16 [16, 128, 128], P('head'), may hold values from -0.5 to 0.5
- samples: int32 [8], replicated, may hold values from 0 to 1
Outputs:
- student: bfloat16 [2048, 16, 128], P('seq', 'head')
- teacher: float32 [8, 128, 16, 128], P('seq', None, 'head')
- loss: float32 [], replicated
Inputs may be any that keep to these rules, and one draw needn't show every extreme that they name: `queries`: query vectors; some may be large multiples of earlier key vectors.
All inputs are finite; a program needn't handle non-finite values.
Results may differ from a plain program's by a relative error of at most 0.009.
Values may be sent and summed in bfloat16 or wider, within the bound.
A program may use at most 64 MiB of HBM per device.

v0:
```python
import jax
import jax.numpy as jnp
from jax import lax
from jax.sharding import PartitionSpec as P

HD = 128
FEAT = 128
QH_DEV = 4
BLOCK = 128


PRECISE = lax.Precision.HIGHEST
MASKED = -1e30


def prefix(x, axis, combine, identity):
    count, mine = (lax.axis_size(axis), lax.axis_index(axis))
    everything = jax.tree.map(
        lambda part, kind: lax.all_gather(part.astype(kind), axis), x, (jnp.bfloat16, jnp.bfloat16)
    )
    start = jax.tree.map(
        lambda part, zero: jnp.broadcast_to(jnp.asarray(zero, part.dtype), part.shape), x, identity
    )

    def lap(k, before):
        reached = k < mine
        new = combine(
            before, jax.tree.map(lambda part, own: part[k].astype(own.dtype), everything, x)
        )
        return jax.tree.map(lambda a, b: jnp.where(reached, a, b), new, before)

    return lax.fori_loop(0, count, lap, start)


def features(logits):
    return jnp.concatenate(
        [jax.nn.softmax(logits, axis=-1), jax.nn.softmax(-logits, axis=-1)], axis=-1
    ).astype(jnp.bfloat16)


def add_pair(earlier, later):
    return (earlier[0] + later[0], earlier[1] + later[1])


def absorb(running, query_rows, row_places, key_part, value_part, inv_root):
    best, totals, accum = running
    scores = (
        jnp.einsum("bhd,kd->hbk", query_rows, key_part, preferred_element_type=jnp.float32)
        * inv_root
    )
    key_places = jnp.arange(key_part.shape[0])
    live = (key_places[None, :] <= row_places[:, None])[None]
    peak = jnp.max(jnp.where(live, scores, MASKED), axis=-1)
    newtop = jnp.maximum(best, peak)
    weights = jnp.where(live, jnp.exp(scores - newtop[..., None]), 0.0)
    totals = jnp.sum(weights, axis=-1)
    accum = jnp.einsum(
        "hbk,kd->hbd", weights.astype(jnp.bfloat16), value_part, preferred_element_type=jnp.float32
    )
    return (newtop, totals, accum)


def on_device(queries, keys, values, feat_q, feat_k, samples):
    tok_rows, head_count, head_width = queries.shape
    stretch_count = lax.axis_size("seq")
    inv_root = 1.0 / head_width**0.5
    key_rows = keys[:, 0]
    value_rows = values[:, 0]
    phi_q = features(
        jnp.einsum("lhd,hdf->lhf", queries, feat_q, preferred_element_type=jnp.float32)
    )
    phi_k = features(
        jnp.einsum("ld,hdf->lhf", key_rows, feat_k, preferred_element_type=jnp.float32)
    )
    span_rows = min(tok_rows, 512)
    block_count = tok_rows // span_rows
    fq_blocks = phi_q.reshape(block_count, span_rows, head_count, 2 * FEAT)
    fk_blocks = phi_k.reshape(block_count, span_rows, head_count, 2 * FEAT)
    value_blocks = value_rows.reshape(block_count, span_rows, head_width)
    block_states = jnp.einsum(
        "nlhf,nld->nhfd", fk_blocks, value_blocks, preferred_element_type=jnp.float32
    )
    block_totals = jnp.sum(fk_blocks, axis=1, dtype=jnp.float32)
    local_state = jnp.sum(block_states, axis=0)
    local_total = jnp.sum(block_totals, axis=0)
    empty_state = jnp.zeros_like(local_state)
    empty_total = jnp.zeros_like(local_total)
    enter_state, enter_total = prefix(
        (local_state, local_total), "seq", add_pair, (empty_state, empty_total)
    )
    before_states = jnp.cumsum(block_states, axis=0) - block_states
    before_totals = jnp.cumsum(block_totals, axis=0) - block_totals
    states_in = enter_state[None] + before_states
    totals_in = enter_total[None] + before_totals
    causal = jnp.arange(span_rows)[:, None] >= jnp.arange(span_rows)[None, :]
    kernel = jnp.einsum("nihf,njhf->nhij", fq_blocks, fk_blocks, preferred_element_type=jnp.float32)
    kernel = jnp.where(causal[None, None], kernel, 0.0)
    kernel_low = kernel.astype(jnp.bfloat16)
    numer = jnp.einsum(
        "nhij,njd->nihd", kernel_low, value_blocks, preferred_element_type=jnp.float32
    )
    numer = numer + jnp.einsum(
        "nihf,nhfd->nihd",
        fq_blocks,
        states_in,
        precision=PRECISE,
        preferred_element_type=jnp.float32,
    )
    denom = jnp.transpose(jnp.sum(kernel, axis=3), (0, 2, 1)) + jnp.einsum(
        "nihf,nhf->nih", fq_blocks, totals_in, precision=PRECISE, preferred_element_type=jnp.float32
    )
    student = (
        (numer / denom[..., None]).astype(jnp.bfloat16).reshape(tok_rows, head_count, head_width)
    )
    device_index = lax.axis_index("seq")
    picked = samples[device_index]
    row_first = device_index * tok_rows + picked * BLOCK
    query_rows = lax.dynamic_slice_in_dim(queries, picked * BLOCK, BLOCK, 0)
    row_places = row_first + jnp.arange(BLOCK)
    fresh = (
        jnp.full((head_count, BLOCK), MASKED, jnp.float32),
        jnp.zeros((head_count, BLOCK), jnp.float32),
        jnp.zeros((head_count, BLOCK, head_width), jnp.float32),
    )
    key_part = lax.all_gather(keys, "seq", axis=0, tiled=True)
    value_part = lax.all_gather(values, "seq", axis=0, tiled=True)
    best, totals, accum = lax.cond(
        jnp.int32(0) <= row_first + BLOCK - 1,
        lambda kept: absorb(
            kept, query_rows, row_places, key_part[:, 0], value_part[:, 0], inv_root
        ),
        lambda kept: kept,
        fresh,
    )
    mixed = accum / totals[..., None]
    teacher = jnp.transpose(mixed, (1, 0, 2))[None]
    student_rows = lax.dynamic_slice_in_dim(student, picked * BLOCK, BLOCK, 0).astype(jnp.float32)
    gap = student_rows - teacher[0]
    entry_count = stretch_count * lax.axis_size("head") * BLOCK * QH_DEV * HD
    loss = lax.psum(jnp.sum(gap * gap), ("seq", "head")) / entry_count
    return (student, teacher, loss)


def solution(mesh):
    in_specs = (
        P("seq", "head", None),
        P("seq", "head", None),
        P("seq", "head", None),
        P("head", None, None),
        P("head", None, None),
        P(),
    )
    out_specs = (P("seq", "head", None), P("seq", None, "head", None), P())
    return jax.shard_map(
        on_device, mesh=mesh, in_specs=in_specs, out_specs=out_specs, check_vma=False
    )
```

profile of v0, /device:TPU:0, one launch (start us, length us, event | category | flops | bytes accessed | tf_op | source)
XLA Modules:
  0.0 174.9 jit_solution(1386197120691396922)
XLA Ops:
  7.2 0.0 copy-start
  7.2 0.0 copy-start.2
  7.2 0.0 copy-start.3
  7.2 0.0 copy-start.4
  7.2 0.0 copy-start.1
  7.2 0.0 all-gather.5.cloned.1.call-start
  7.3 1.1 copy.23
  8.4 1.1 fusion.43
  9.5 1.2 fusion.61
  10.7 0.5 fusion.64
  11.2 0.1 divide_convert_fusion
  11.3 0.0 copy-done.3
  11.3 1.0 fusion.65
  12.3 0.0 all-gather.5.cloned.1.call-update
  12.3 0.0 copy-done.4
  12.3 0.6 dynamic_slice.26
  13.6 0.0 copy-done.2
  13.6 33.7 %all_gather.16 = bf16[2048,1,128]{2,0,1:T(8,128)(2,1)S(1)} all-gather(bf16[256,1,128]{2,0,1:T(8,128)(2,1)S(1)} %copy-done.2), channel_id=1, replica_groups=mesh['seq'=8,'head'=4] {'seq'}, dimensions={0}, use_global_device_ids=true | all-gather | bytes 589824 | tf_op jit(solution)/shard_map/all_gather | solution.py:125
  47.3 32.5 %all_gather.17 = bf16[2048,1,128]{2,0,1:T(8,128)(2,1)S(1)} all-gather(bf16[256,1,128]{2,0,1:T(8,128)(2,1)S(1)} %copy-done.3), channel_id=1, replica_groups=mesh['seq'=8,'head'=4] {'seq'}, dimensions={0}, use_global_device_ids=true | all-gather | bytes 589824 | tf_op jit(solution)/shard_map/all_gather | solution.py:126
  79.9 3.4 %conditional.1 = (f32[4,128]{1,0:T(4,128)S(1)}, f32[4,128,128]{2,1,0:T(8,128)S(1)}) conditional(s32[]{:T(128)} %convert_element_type.94, () %tuple.33, (s32[]{:T(128)}, s32[128]{0:T(128)S(1)}, bf16[256,4,128]{2,1,0:T(4,128)(2,1)S(1)}, s32[]{:T(128)}, bf16[2048,1,128]{2,0,1:T(8,128)(2,1)S(1)}, /*index=5*/bf16[2048,1,128]{2,0,1:T(8,128)(2,1)S(1)}) %tuple.69), branch_computations={%region_12.13_spmd, %region_13.0_spmd} | conditional | flops 548667008 | bytes 15611416 | solution.py:127
  79.9 0.2 iota_compare_fusion
  80.1 1.0 fusion
  81.2 1.0 fusion.5
  82.1 1.2 fusion.4
  83.3 0.2 convert_reduce_fusion
  83.5 26.0 %all-gather.2 = bf16[8,4,256]{2,1,0:T(4,128)(2,1)S(1)} all-gather(bf16[1,4,256]{2,1,0:T(4,128)(2,1)S(1)} %convert_bitcast_fusion), channel_id=3, replica_groups=mesh['seq'=8,'head'=4] {'seq'}, dimensions={0}, use_global_device_ids=true | all-gather | bytes 18432 | tf_op jit(solution)/shard_map/all_gather | solution.py:19
  109.6 0.1 fusion.40
  109.7 1.2 fusion.66
  110.9 0.4 fusion.69
  111.2 1.1 divide_convert_fusion.2
  112.4 0.4 fusion.72
  112.7 0.0 all-gather.5.cloned.1.call-done
  112.8 10.2 %while.16 = (s32[]{:T(128)}, f32[4,256,128]{2,1,0:T(8,128)S(1)}, f32[4,256]{1,0:T(4,128)S(1)}, s32[]{:T(128)}, bf16[8,4,256,128]{3,2,1,0:T(8,128)(2,1)}, /*index...) while((s32[]{:T(128)}, f32[4,256,128]{2,1,0:T(8,128)S(1)}, f32[4,256]{1,0:T(4,128)S(1)}, ...), condition=%wide.region_10.0_spmd.clone, body=%wide.region_9.0_spmd.clone.sunk | while | flops 528388 | bytes 1321075 | solution.py:32
  112.8 1.2 add_select_fusion.4
  114.1 1.2 add_select_fusion.4
  115.3 1.2 add_select_fusion.4
  116.6 1.2 add_select_fusion.4
  117.9 1.2 add_select_fusion.4
  119.2 1.2 add_select_fusion.4
  120.4 1.2 add_select_fusion.4
  121.7 1.2 add_select_fusion.4
  123.0 0.3 fusion.39
  123.3 0.7 convolution_bitcast_fusion.2
  124.0 0.4 fusion.29
  124.4 0.7 fusion.37
  125.2 0.9 copy.32
  126.0 39.3 %psum.7 = f32[]{:T(128)} all-reduce(f32[]{:T(128)} %fusion.37), channel_id=1, replica_groups=mesh['seq'=8,'head'=4] {'seq','head'}, use_global_device_ids=true, to_apply=%region_17.18 | all-reduce | flops 1 | bytes 8 | tf_op jit(solution)/shard_map/psum | solution.py:140
  165.4 0.9 copy.31
  (20 shorter events, 0.2 us)
Async XLA Ops:
  7.2 102.5 %copy-start = (bf16[4,128,128]{2,1,0:T(8,128)(2,1)S(1)}, bf16[4,128,128]{2,1,0:T(8,128)(2,1)}, u32[]{:S(2)}) copy-start(bf16[4,128,128]{2,1,0:T(8,128)(2,1)} %param.13) | copy-start | bytes 393220
  7.2 6.4 %copy-start.2 = (bf16[256,1,128]{2,0,1:T(8,128)(2,1)S(1)}, bf16[256,1,128]{2,0,1:T(8,128)(2,1)}, u32[]{:S(2)}) copy-start(bf16[256,1,128]{2,0,1:T(8,128)(2,1)} %param.11) | copy-start | bytes 196612
  7.2 4.1 %copy-start.3 = (bf16[256,1,128]{2,0,1:T(8,128)(2,1)S(1)}, bf16[256,1,128]{2,0,1:T(8,128)(2,1)}, u32[]{:S(2)}) copy-start(bf16[256,1,128]{2,0,1:T(8,128)(2,1)} %param.12) | copy-start | bytes 196612
  7.2 5.1 %copy-start.4 = (s32[8]{0:T(128)S(1)}, s32[8]{0:T(128)}, u32[]{:S(2)}) copy-start(s32[8]{0:T(128)} %param.15) | copy-start | bytes 100
  7.2 72.7 %copy-start.1 = (bf16[256,4,128]{2,1,0:T(4,128)(2,1)S(1)}, bf16[256,4,128]{2,1,0:T(4,128)(2,1)}, u32[]{:S(2)}) copy-start(bf16[256,4,128]{2,1,0:T(4,128)(2,1)} %param.10) | copy-start | bytes 786436
  7.2 105.5 %all-gather.5.cloned.1.call-start = ((), (), s32[]{:S(2)}) async-start(), calls=%async_computation | async-start | bytes 2359296 | tf_op jit(solution)/shard_map/all_gather | solution.py:19
Sparse Core Ops, SparseCore 0:
  12.4 59.2 all-gather.4
where the time goes:
time: 176 us; the launch traced here: 175 us
  blocking collectives  132 us (75%)
  between operations  16.6 us (9%)
  other arithmetic  14.3 us (8%)
  matrix products  8.52 us (5%)
  local copies, waits for them, and re-layouts  3.57 us (2%)
    psum x1, blocking collectives, on_device(): loss = lax.psum(jnp.sum(gap * gap), ('seq', 'head')) / entry_count  39.3 us
    all_gather x1, blocking collectives, on_device(): key_part = lax.all_gather(keys, 'seq', axis=0, tiled=True)  33.7 us
    all_gather x1, blocking collectives, on_device(): value_part = lax.all_gather(values, 'seq', axis=0, tiled=True)  32.5 us
    all_gather x1, blocking collectives, prefix(): lax.all_gather(part.astype(kind), axis)  26 us
    select_n x16, other arithmetic, lap(): return jax.tree.map(lambda a, b: jnp.where(reached, a, b), new, before)  10 us
  transfers between devices with their start and end apart: 1, of which 0 were waited for; matrix products, arithmetic and copies ran while one was open for 4% of the time, Pallas kernels for 0%

commit v1 on v0

v1 whole, which is shorter than its diff:
```python
import functools

import jax
import jax.numpy as jnp
from jax import lax
from jax.experimental import pallas as pl
from jax.experimental.pallas import tpu as pltpu
from jax.sharding import PartitionSpec as P

BLOCK = 128
MASKED = -1e30
LOG2E = 1.4426950408889634
NT = (((1,), (1,)), ((), ()))


def dot(a, b):
    return jnp.dot(a, b, preferred_element_type=jnp.float32)


def soft_pair(logits, axis):
    up = jnp.exp(logits - jnp.max(logits, axis=axis, keepdims=True))
    down = jnp.exp(jnp.min(logits, axis=axis, keepdims=True) - logits)
    up = up * (1.0 / jnp.sum(up, axis=axis, keepdims=True))
    down = down * (1.0 / jnp.sum(down, axis=axis, keepdims=True))
    return jnp.concatenate([up, down], axis=axis).astype(jnp.bfloat16)


def kernel(
    n, nh, q_hbm, k_hbm, v_hbm, fq_hbm, fk_hbm, samples, student, teacher, loss,
    kv, q_raw, fq, fk, fk_t, rows32, qs_t, phi_q, state, num, den, top, tot, acc, out32, heads_part, seq_part,
    local_sem, recv_sem, send_sem, head_send, head_recv, seq_send, seq_recv,
):
    tok, width = k_hbm.shape
    heads = fq.shape[0]
    s, hd = lax.axis_index("seq"), lax.axis_index("head")
    outer, y = s // 2, s % 2
    last = n // 2 - 1
    partner = s + 1 - 2 * y
    own = (k_hbm, v_hbm)

    local = [
        pltpu.make_async_copy(src, dst, local_sem.at[i])
        for i, (src, dst) in enumerate(
            [(q_hbm, q_raw), (fq_hbm, fq), (fk_hbm, fk), (k_hbm, kv.at[s, 0]), (v_hbm, kv.at[s, 1])]
        )
    ]
    for copy in local:
        copy.start()

    barrier = pltpu.get_barrier_semaphore()
    for i in range(1, n):
        pl.semaphore_signal(barrier, inc=1, device_id={"seq": lax.rem(s + i, n)}, device_id_type=pl.DeviceIdType.MESH)
    for i in range(1, nh):
        pl.semaphore_signal(barrier, inc=1, device_id={"head": lax.rem(hd + i, nh)}, device_id_type=pl.DeviceIdType.MESH)
    pl.semaphore_wait(barrier, n - 1 + nh - 1)

    def hop(src, slot, j, way, target):
        return pltpu.make_async_remote_copy(
            src_ref=src, dst_ref=kv.at[slot, j], send_sem=send_sem.at[way, slot, j],
            recv_sem=recv_sem.at[slot, j], device_id={"seq": target}, device_id_type=pl.DeviceIdType.MESH,
        )

    @pl.when(outer < last)
    def _():
        for j in range(2):
            hop(own[j], s, j, 0, s + 2).start()

    @pl.when(y == 0)
    def _():
        for j in range(2):
            hop(own[j], s, j, 1, partner).start()

    pick = samples[s]

    def chosen(rows):
        block = rows[:BLOCK]
        for b in range(1, tok // BLOCK):
            block = jnp.where(pick == b, rows[b * BLOCK:(b + 1) * BLOCK], block)
        return block

    def key_features(keys, h):
        logits = lax.dot_general(fk_t[h * 128:(h + 1) * 128, :], keys, NT, preferred_element_type=jnp.float32)
        return soft_pair(logits, 0)

    def teach(keys, values, live):
        values_t = values.astype(jnp.float32).T.astype(jnp.bfloat16)
        for c in range(heads // 2):
            cols = slice(c * 2 * BLOCK, (c + 1) * 2 * BLOCK)
            scores = dot(keys, qs_t[:, cols]) * (LOG2E / width ** 0.5)
            if live is not None:
                scores = jnp.where(live, scores, MASKED)
            peak = jnp.max(scores, axis=0, keepdims=True)
            if live is None:
                old = top[:, cols]
                peak = jnp.maximum(old, peak)
                fade = jnp.exp2(old - peak)
            weights = jnp.exp2(scores - peak)
            total = jnp.sum(weights, axis=0, keepdims=True)
            mixed = dot(values_t, weights.astype(jnp.bfloat16))
            if live is None:
                total = total + tot[:, cols] * fade
                mixed = mixed + acc[:, cols] * fade
            top[:, cols] = peak
            tot[:, cols] = total
            acc[:, cols] = mixed

    def wide(values):
        return jnp.concatenate([values, jnp.ones_like(values)], axis=1)

    def absorb(slot):
        keys, values = kv[slot, 0], kv[slot, 1]
        teach(keys, values, None)
        values_wide = wide(values)
        for h in range(heads):
            state[h] += dot(key_features(keys, h), values_wide)

    state[...] = jnp.zeros_like(state)
    for copy in local:
        copy.wait()
    rows32[...] = q_raw[...].astype(jnp.float32)
    for h in range(heads):
        mine = rows32[pl.ds(h, tok, stride=heads), :]
        qs_t[:, h * BLOCK:(h + 1) * BLOCK] = chosen(mine).T.astype(jnp.bfloat16)
        fk_t[h * 128:(h + 1) * 128, :] = fk[h].astype(jnp.float32).T.astype(jnp.bfloat16)
        phi_q[h] = soft_pair(dot(mine.astype(jnp.bfloat16), fq[h]), 1)
    keys, values = kv[s, 0], kv[s, 1]
    place = lax.broadcasted_iota(jnp.int32, (tok, 2 * BLOCK), 0)
    row = lax.broadcasted_iota(jnp.int32, (tok, 2 * BLOCK), 1) % BLOCK + pick * BLOCK
    teach(keys, values, place <= row)
    causal = lax.broadcasted_iota(jnp.int32, (tok, tok), 0) >= lax.broadcasted_iota(jnp.int32, (tok, tok), 1)
    for h in range(heads):
        inner = jnp.where(causal, dot(phi_q[h], key_features(keys, h)), 0.0)
        num[h] = dot(inner.astype(jnp.bfloat16), values)
        den[h] = jnp.broadcast_to(jnp.sum(inner, axis=1, keepdims=True), (tok, width))

    @pl.when(y == 1)
    def _():
        for j in range(2):
            hop(own[j], partner, j, 1, partner).wait_recv()
        absorb(partner)

    def lap(d, carry):
        near, far = s - 2 * d, partner - 2 * d
        for j in range(2):
            hop(kv.at[near, j], near, j, 0, s).wait_recv()

            @pl.when(outer < last)
            def _():
                hop(kv.at[near, j], near, j, 0, s + 2).start()

            hop(kv.at[near, j], near, j, 1, partner).start()
        absorb(near)
        for j in range(2):
            hop(kv.at[far, j], far, j, 1, partner).wait_recv()
        absorb(far)
        return carry

    lax.fori_loop(1, outer + 1, lap, 0)

    part = jnp.zeros((8, width), jnp.float32)
    for h in range(heads):
        cols = slice(h * BLOCK, (h + 1) * BLOCK)
        inter = dot(phi_q[h], state[h].astype(jnp.bfloat16))
        result = (num[h] + inter[:, :width]) / (den[h] + inter[:, width:])
        result = result.astype(jnp.bfloat16).astype(jnp.float32)
        out32[pl.ds(h, tok, stride=heads), :] = result
        mixed = (acc[:, cols] / tot[:, cols]).T
        teacher[pl.ds(h, BLOCK, stride=heads), :] = mixed
        gap = chosen(result) - mixed
        part = part + jnp.sum((gap * gap).reshape(BLOCK // 8, 8, width), axis=0)

    def spread(buf, mine, count, axis, send, recv, i):
        return pltpu.make_async_remote_copy(
            src_ref=buf.at[mine], dst_ref=buf.at[mine], send_sem=send.at[i], recv_sem=recv.at[i],
            device_id={axis: lax.rem(mine + i, count)}, device_id_type=pl.DeviceIdType.MESH,
        )

    heads_part[hd] = part
    copies = [spread(heads_part, hd, nh, "head", head_send, head_recv, i) for i in range(1, nh)]
    for copy in copies:
        copy.start()
    student[...] = out32[...].astype(jnp.bfloat16)
    for copy in copies:
        copy.wait()
    seq_part[s] = jnp.sum(heads_part[...], axis=0)
    copies = [spread(seq_part, s, n, "seq", seq_send, seq_recv, i) for i in range(1, n)]
    for copy in copies:
        copy.start()

    @pl.when(outer < last)
    def _():
        for j in range(2):
            hop(own[j], s, j, 0, s + 2).wait_send()

    @pl.when(y == 0)
    def _():
        for j in range(2):
            hop(own[j], s, j, 1, partner).wait_send()

    def drain(d, carry):
        near = s - 2 * d
        for j in range(2):
            @pl.when(outer < last)
            def _():
                hop(kv.at[near, j], near, j, 0, s + 2).wait_send()

            hop(kv.at[near, j], near, j, 1, partner).wait_send()
        return carry

    lax.fori_loop(1, outer + 1, drain, 0)
    for copy in copies:
        copy.wait()
    loss[0, 0] = jnp.sum(seq_part[...]) * (1.0 / (n * nh * BLOCK * heads * width))


def on_device(n, nh, queries, keys, values, feat_q, feat_k, samples):
    tok, heads, width = queries.shape
    bf16, f32 = jnp.bfloat16, jnp.float32
    anywhere = pl.BlockSpec(memory_space=pl.ANY)
    in_vmem = pl.BlockSpec(memory_space=pltpu.VMEM)
    in_smem = pl.BlockSpec(memory_space=pltpu.SMEM)
    dma = pltpu.SemaphoreType.DMA
    student, teacher, loss = pl.pallas_call(
        functools.partial(kernel, n, nh),
        out_shape=(
            jax.ShapeDtypeStruct((tok * heads, width), bf16),
            jax.ShapeDtypeStruct((BLOCK * heads, width), f32),
            jax.ShapeDtypeStruct((1, 1), f32),
        ),
        in_specs=[anywhere] * 5 + [in_smem],
        out_specs=(in_vmem, in_vmem, in_smem),
        scratch_shapes=[
            pltpu.VMEM((n, 2, tok, width), bf16),
            pltpu.VMEM((tok * heads, width), bf16),
            pltpu.VMEM(feat_q.shape, bf16),
            pltpu.VMEM(feat_k.shape, bf16),
            pltpu.VMEM((heads * 128, width), bf16),
            pltpu.VMEM((tok * heads, width), f32),
            pltpu.VMEM((width, heads * BLOCK), bf16),
            pltpu.VMEM((heads, tok, 256), bf16),
            pltpu.VMEM((heads, 256, 2 * width), f32),
            pltpu.VMEM((heads, tok, width), f32),
            pltpu.VMEM((heads, tok, width), f32),
            pltpu.VMEM((1, heads * BLOCK), f32),
            pltpu.VMEM((1, heads * BLOCK), f32),
            pltpu.VMEM((width, heads * BLOCK), f32),
            pltpu.VMEM((tok * heads, width), f32),
            pltpu.VMEM((nh, 8, width), f32),
            pltpu.VMEM((n, 8, width), f32),
            dma((5,)), dma((n, 2)), dma((2, n, 2)), dma((nh,)), dma((nh,)), dma((n,)), dma((n,)),
        ],
        compiler_params=pltpu.CompilerParams(
            collective_id=0, has_side_effects=True, vmem_limit_bytes=60 * 1024 * 1024
        ),
    )(
        queries.reshape(tok * heads, width), keys.reshape(tok, width), values.reshape(tok, width),
        feat_q, feat_k, samples,
    )
    return student.reshape(tok, heads, width), teacher.reshape(1, BLOCK, heads, width), loss.reshape(())


def solution(mesh):
    in_specs = (
        P("seq", "head", None),
        P("seq", "head", None),
        P("seq", "head", None),
        P("head", None, None),
        P("head", None, None),
        P(),
    )
    out_specs = (P("seq", "head", None), P("seq", None, "head", None), P())
    return jax.shard_map(
        functools.partial(on_device, mesh.shape["seq"], mesh.shape["head"]),
        mesh=mesh, in_specs=in_specs, out_specs=out_specs, check_vma=False,
    )
```

time: 176 us -> 41.1 us (0.23)
  blocking collectives: 132 us -> 0 us
  Pallas kernels: 0 us -> 36.1 us
  other arithmetic: 14.3 us -> 0 us
  between operations: 16.6 us -> 2.41 us
  matrix products: 8.52 us -> 0 us
    all_gather x3 -> x0, blocking collectives: 92.3 us -> none  [the longest x1 33.7 us: on_device(): key_part = lax.all_gather(keys, 'seq', axis=0, tiled=True)]
    psum x1 -> x0, blocking collectives: 39.3 us -> none  [on_device(): loss = lax.psum(jnp.sum(gap * gap), ('seq', 'head')) / entry_count]
    pallas_call x0 -> x1, Pallas kernels: none -> 36.1 us  [on_device(): pl.pallas_call(functools.partial(kernel, n, nh), out_shape=(jax.ShapeDtyp...]
    select_n x16 -> x0, other arithmetic: 10 us -> none  [lap(): return jax.tree.map(lambda a, b: jnp.where(reached, a, b), new, before)]
    dot_general x7 -> x0, matrix products: 4.75 us -> none  [the longest x1 1.01 us: absorb(): jnp.einsum('bhd,kd->hbk', query_rows, key_part, preferred_element_type=jn...]
    sub x3 -> x0, matrix products: 2.7 us -> none  [the longest x2 2.34 us: features(): jax.nn.softmax(-logits, axis=-1)]
    reduce_sum x3 -> x0, other arithmetic: 2.12 us -> none  [the longest x1 1.15 us: absorb(): totals = jnp.sum(weights, axis=-1)]
  transfers between devices with their start and end apart: 1 -> 0, of which waited for: 0 -> 0; matrix products, arithmetic and copies ran while one was open for 4% -> 0% of each run, Pallas kernels for 0% -> 0%
where the time goes in v1:
time: 41.1 us; the launch traced here: 41 us
  Pallas kernels  36.1 us (88%)
  local copies, waits for them, and re-layouts  2.49 us (6%)
  between operations  2.41 us (6%)
    pallas_call x1, Pallas kernels, on_device(): pl.pallas_call(functools.partial(kernel, n, nh), out_shape=(jax.ShapeDtyp...  36.1 us
    unnamed x4, local copies, waits for them, and re-layouts  2.49 us

profile of v1, /device:TPU:0, one launch (start us, length us, event | category | flops | bytes accessed | tf_op | source)
XLA Modules:
  0.0 41.0 jit_solution(4438703957921814578)
XLA Ops:
  0.6 36.1 %shard_map.85 = (bf16[1024,128]{1,0:T(8,128)(2,1)}, f32[512,128]{1,0:T(8,128)}, f32[1,1]{1,0:T(1,128)}) custom-call(bf16[1024,128]{1,0:T(8,128)(2,1)} %bitcast.6, bf16[256,128]{1,0:T(8,128)(2,1)} %bitcast.9, bf16[256,128]{1,0:T(8,128)(2,1)} %bitcast.10, bf16[4,128,128]{2,1,0:T(8,128)(2,1)} %fq_hbm.1, bf16[4,128,128]{2,1,0:T(8,128)(2,1)} %fk_hbm.1, s32[8]{0:T(128)} %samples.1), custom_call_target="tpu_custom_call" | custom-call | tf_op jit(solution)/shard_map/pallas_call | solution.py:223
  36.7 0.0 copy-start
  36.7 1.8 %copy.12 = bf16[256,4,128]{2,1,0:T(4,128)(2,1)} copy(bf16[256,4,128]{2,1,0:T(4,128)(2,1)} %bitcast.8) | data formatting | bytes 524288
  38.5 0.0 copy-done
  38.5 0.7 %copy.13 = f32[1,128,4,128]{3,2,1,0:T(4,128)} copy(f32[1,128,4,128]{3,2,1,0:T(4,128)S(1)} %bitcast.7) | data formatting | bytes 524288
Async XLA Ops:
  36.7 1.8 %copy-start = (f32[512,128]{1,0:T(8,128)S(1)}, f32[512,128]{1,0:T(8,128)}, u32[]{:S(2)}) copy-start(f32[512,128]{1,0:T(8,128)} %get-tuple-element.7) | copy-start | bytes 786436

commit v2 on v1

--- a/solution.py
+++ b/solution.py
@@ -26,9 +26,9 @@
 
 
 def kernel(
-    n, nh, q_hbm, k_hbm, v_hbm, fq_hbm, fk_hbm, samples, student, teacher, loss,
-    kv, q_raw, fq, fk, fk_t, rows32, qs_t, phi_q, state, num, den, top, tot, acc, out32, heads_part, seq_part,
-    local_sem, recv_sem, send_sem, head_send, head_recv, seq_send, seq_recv,
+    n, nh, q_hbm, k_hbm, v_hbm, fq_hbm, fk_hbm, samples, out32, teacher, loss,
+    kv, q_raw, fq, fk, fk_t, rows32, qs_t, phi_q, state, num, den, top, tot, acc, column, below, plane, total,
+    local_sem, recv_sem, send_sem, up_sem, plane_send, plane_recv, down_send, down_recv,
 ):
     tok, width = k_hbm.shape
     heads = fq.shape[0]
@@ -48,11 +48,24 @@
         copy.start()
 
     barrier = pltpu.get_barrier_semaphore()
-    for i in range(1, n):
-        pl.semaphore_signal(barrier, inc=1, device_id={"seq": lax.rem(s + i, n)}, device_id_type=pl.DeviceIdType.MESH)
-    for i in range(1, nh):
-        pl.semaphore_signal(barrier, inc=1, device_id={"head": lax.rem(hd + i, nh)}, device_id_type=pl.DeviceIdType.MESH)
-    pl.semaphore_wait(barrier, n - 1 + nh - 1)
+    mate = y * nh + hd
+
+    def plane_device(i):
+        other = lax.rem(mate + i, 2 * nh)
+        return {"seq": 2 * outer + other // nh, "head": lax.rem(other, nh)}
+
+    for i in range(1, 2 * nh):
+        pl.semaphore_signal(barrier, inc=1, device_id=plane_device(i), device_id_type=pl.DeviceIdType.MESH)
+
+    @pl.when(outer > 0)
+    def _():
+        pl.semaphore_signal(barrier, inc=1, device_id={"seq": s - 2}, device_id_type=pl.DeviceIdType.MESH)
+
+    @pl.when(outer < last)
+    def _():
+        pl.semaphore_signal(barrier, inc=1, device_id={"seq": s + 2}, device_id_type=pl.DeviceIdType.MESH)
+
+    pl.semaphore_wait(barrier, 2 * nh - 1 + jnp.minimum(outer, 1) + jnp.minimum(last - outer, 1))
 
     def hop(src, slot, j, way, target):
         return pltpu.make_async_remote_copy(
@@ -82,37 +95,58 @@
         logits = lax.dot_general(fk_t[h * 128:(h + 1) * 128, :], keys, NT, preferred_element_type=jnp.float32)
         return soft_pair(logits, 0)
 
-    def teach(keys, values, live):
-        values_t = values.astype(jnp.float32).T.astype(jnp.bfloat16)
+    def weigh(keys, live):
+        out = []
         for c in range(heads // 2):
             cols = slice(c * 2 * BLOCK, (c + 1) * 2 * BLOCK)
             scores = dot(keys, qs_t[:, cols]) * (LOG2E / width ** 0.5)
             if live is not None:
                 scores = jnp.where(live, scores, MASKED)
             peak = jnp.max(scores, axis=0, keepdims=True)
+            fade = None
             if live is None:
                 old = top[:, cols]
                 peak = jnp.maximum(old, peak)
                 fade = jnp.exp2(old - peak)
             weights = jnp.exp2(scores - peak)
-            total = jnp.sum(weights, axis=0, keepdims=True)
-            mixed = dot(values_t, weights.astype(jnp.bfloat16))
-            if live is None:
-                total = total + tot[:, cols] * fade
-                mixed = mixed + acc[:, cols] * fade
+            part = jnp.sum(weights, axis=0, keepdims=True)
             top[:, cols] = peak
-            tot[:, cols] = total
-            acc[:, cols] = mixed
-
-    def wide(values):
-        return jnp.concatenate([values, jnp.ones_like(values)], axis=1)
-
-    def absorb(slot):
-        keys, values = kv[slot, 0], kv[slot, 1]
-        teach(keys, values, None)
-        values_wide = wide(values)
+            tot[:, cols] = part if live is not None else part + tot[:, cols] * fade
+            out.append((cols, weights.astype(jnp.bfloat16), fade))
+        return out
+
+    def mix(weighed, values):
+        values_t = values.astype(jnp.float32).T.astype(jnp.bfloat16)
+        for cols, weights, fade in weighed:
+            mixed = dot(values_t, weights)
+            acc[:, cols] = mixed if fade is None else mixed + acc[:, cols] * fade
+
+    def arrived(slot, j):
+        hop(kv.at[slot, j], slot, j, 0, partner).wait_recv()
+
+    def absorb(slot, wait):
+        if wait:
+            arrived(slot, 0)
+        keys = kv[slot, 0]
+        weighed = weigh(keys, None)
+        features = [key_features(keys, h) for h in range(heads)]
+        if wait:
+            arrived(slot, 1)
+        values = kv[slot, 1]
+        mix(weighed, values)
+        values_wide = jnp.concatenate([values, jnp.ones_like(values)], axis=1)
         for h in range(heads):
-            state[h] += dot(key_features(keys, h), values_wide)
+            state[h] += dot(features[h], values_wide)
+
+    def relay(slot):
+        for j in range(2):
+            arrived(slot, j)
+
+            @pl.when(outer < last)
+            def _():
+                hop(kv.at[slot, j], slot, j, 0, s + 2).start()
+
+            hop(kv.at[slot, j], slot, j, 1, partner).start()
 
     state[...] = jnp.zeros_like(state)
     for copy in local:
@@ -123,10 +157,15 @@
         qs_t[:, h * BLOCK:(h + 1) * BLOCK] = chosen(mine).T.astype(jnp.bfloat16)
         fk_t[h * 128:(h + 1) * 128, :] = fk[h].astype(jnp.float32).T.astype(jnp.bfloat16)
         phi_q[h] = soft_pair(dot(mine.astype(jnp.bfloat16), fq[h]), 1)
+
+    @pl.when(outer > 0)
+    def _():
+        relay(s - 2)
+
     keys, values = kv[s, 0], kv[s, 1]
     place = lax.broadcasted_iota(jnp.int32, (tok, 2 * BLOCK), 0)
     row = lax.broadcasted_iota(jnp.int32, (tok, 2 * BLOCK), 1) % BLOCK + pick * BLOCK
-    teach(keys, values, place <= row)
+    mix(weigh(keys, place <= row), values)
     causal = lax.broadcasted_iota(jnp.int32, (tok, tok), 0) >= lax.broadcasted_iota(jnp.int32, (tok, tok), 1)
     for h in range(heads):
         inner = jnp.where(causal, dot(phi_q[h], key_features(keys, h)), 0.0)
@@ -135,24 +174,16 @@
 
     @pl.when(y == 1)
     def _():
-        for j in range(2):
-            hop(own[j], partner, j, 1, partner).wait_recv()
-        absorb(partner)
+        absorb(partner, True)
 
     def lap(d, carry):
-        near, far = s - 2 * d, partner - 2 * d
-        for j in range(2):
-            hop(kv.at[near, j], near, j, 0, s).wait_recv()
-
-            @pl.when(outer < last)
-            def _():
-                hop(kv.at[near, j], near, j, 0, s + 2).start()
-
-            hop(kv.at[near, j], near, j, 1, partner).start()
-        absorb(near)
-        for j in range(2):
-            hop(kv.at[far, j], far, j, 1, partner).wait_recv()
-        absorb(far)
+        absorb(s - 2 * d, False)
+
+        @pl.when(d < outer)
+        def _():
+            relay(s - 2 * d - 2)
+
+        absorb(partner - 2 * d, True)
         return carry
 
     lax.fori_loop(1, outer + 1, lap, 0)
@@ -169,23 +200,41 @@
         gap = chosen(result) - mixed
         part = part + jnp.sum((gap * gap).reshape(BLOCK // 8, 8, width), axis=0)
 
-    def spread(buf, mine, count, axis, send, recv, i):
+    def send(src, dst, send_sem, recv_sem, device):
         return pltpu.make_async_remote_copy(
-            src_ref=buf.at[mine], dst_ref=buf.at[mine], send_sem=send.at[i], recv_sem=recv.at[i],
-            device_id={axis: lax.rem(mine + i, count)}, device_id_type=pl.DeviceIdType.MESH,
+            src_ref=src, dst_ref=dst, send_sem=send_sem, recv_sem=recv_sem,
+            device_id=device, device_id_type=pl.DeviceIdType.MESH,
         )
 
-    heads_part[hd] = part
-    copies = [spread(heads_part, hd, nh, "head", head_send, head_recv, i) for i in range(1, nh)]
-    for copy in copies:
-        copy.start()
-    student[...] = out32[...].astype(jnp.bfloat16)
-    for copy in copies:
-        copy.wait()
-    seq_part[s] = jnp.sum(heads_part[...], axis=0)
-    copies = [spread(seq_part, s, n, "seq", seq_send, seq_recv, i) for i in range(1, n)]
-    for copy in copies:
-        copy.start()
+    upward = send(column, below, up_sem.at[0], up_sem.at[1], {"seq": s + 2})
+    across = [
+        send(plane.at[mate], plane.at[mate], plane_send.at[i], plane_recv.at[i], plane_device(i))
+        for i in range(1, 2 * nh)
+    ]
+    downward = [
+        send(total, total, down_send.at[i], down_recv.at[0], {"seq": s - 2 * i}) for i in range(1, last + 1)
+    ]
+    column[...] = part
+
+    @pl.when(outer > 0)
+    def _():
+        upward.wait_recv()
+        column[...] += below[...]
+
+    @pl.when(outer < last)
+    def _():
+        upward.start()
+
+    @pl.when(outer == last)
+    def _():
+        plane[mate] = column[...]
+        for copy in across:
+            copy.start()
+        for copy in across:
+            copy.wait()
+        total[...] = jnp.sum(plane[...], axis=0)
+        for copy in downward:
+            copy.start()
 
     @pl.when(outer < last)
     def _():
@@ -208,9 +257,18 @@
         return carry
 
     lax.fori_loop(1, outer + 1, drain, 0)
-    for copy in copies:
-        copy.wait()
-    loss[0, 0] = jnp.sum(seq_part[...]) * (1.0 / (n * nh * BLOCK * heads * width))
+
+    @pl.when(outer == last)
+    def _():
+        for copy in downward:
+            copy.wait_send()
+
+    @pl.when(outer < last)
+    def _():
+        upward.wait_send()
+        downward[0].wait_recv()
+
+    loss[0, 0] = jnp.sum(total[...]) * (1.0 / (n * nh * BLOCK * heads * width))
 
 
 def on_device(n, nh, queries, keys, values, feat_q, feat_k, samples):
@@ -223,7 +281,7 @@
     student, teacher, loss = pl.pallas_call(
         functools.partial(kernel, n, nh),
         out_shape=(
-            jax.ShapeDtypeStruct((tok * heads, width), bf16),
+            jax.ShapeDtypeStruct((tok * heads, width), f32),
             jax.ShapeDtypeStruct((BLOCK * heads, width), f32),
             jax.ShapeDtypeStruct((1, 1), f32),
         ),
@@ -244,10 +302,11 @@
             pltpu.VMEM((1, heads * BLOCK), f32),
             pltpu.VMEM((1, heads * BLOCK), f32),
             pltpu.VMEM((width, heads * BLOCK), f32),
-            pltpu.VMEM((tok * heads, width), f32),
-            pltpu.VMEM((nh, 8, width), f32),
-            pltpu.VMEM((n, 8, width), f32),
-            dma((5,)), dma((n, 2)), dma((2, n, 2)), dma((nh,)), dma((nh,)), dma((n,)), dma((n,)),
+            pltpu.VMEM((8, width), f32),
+            pltpu.VMEM((8, width), f32),
+            pltpu.VMEM((2 * nh, 8, width), f32),
+            pltpu.VMEM((8, width), f32),
+            dma((5,)), dma((n, 2)), dma((2, n, 2)), dma((2,)), dma((2 * nh,)), dma((2 * nh,)), dma((n // 2,)), dma((1,)),
         ],
         compiler_params=pltpu.CompilerParams(
             collective_id=0, has_side_effects=True, vmem_limit_bytes=60 * 1024 * 1024
@@ -256,7 +315,7 @@
         queries.reshape(tok * heads, width), keys.reshape(tok, width), values.reshape(tok, width),
         feat_q, feat_k, samples,
     )
-    return student.reshape(tok, heads, width), teacher.reshape(1, BLOCK, heads, width), loss.reshape(())
+    return student.reshape(tok, heads, width).astype(bf16), teacher.reshape(1, BLOCK, heads, width), loss.reshape(())
 
 
 def solution(mesh):

time: 41.1 us -> 35.3 us (0.86)
  Pallas kernels: 36.1 us -> 30.2 us
  other arithmetic: 0 us -> 1.81 us
  local copies, waits for them, and re-layouts: 2.49 us -> 0.71 us
    pallas_call x1, Pallas kernels: 36.1 us -> 30.2 us  [on_device(): pl.pallas_call(functools.partial(kernel, n, nh), out_shape=(jax.ShapeDtyp...]
    convert_element_type x0 -> x1, other arithmetic: none -> 1.81 us  [on_device(): student.reshape(tok, heads, width).astype(bf16)]
    unnamed x4 -> x3, local copies, waits for them, and re-layouts: 2.49 us -> 0.71 us
where the time goes in v2:
time: 35.3 us; the launch traced here: 35.2 us
  Pallas kernels  30.2 us (86%)
  between operations  2.41 us (7%)
  other arithmetic  1.81 us (5%)
  local copies, waits for them, and re-layouts  0.71 us (2%)
    pallas_call x1, Pallas kernels, on_device(): pl.pallas_call(functools.partial(kernel, n, nh), out_shape=(jax.ShapeDtyp...  30.2 us
    convert_element_type x1, other arithmetic, on_device(): student.reshape(tok, heads, width).astype(bf16)  1.81 us
    unnamed x3, local copies, waits for them, and re-layouts  0.71 us

profile of v2, /device:TPU:0, one launch (start us, length us, event | category | flops | bytes accessed | tf_op | source)
XLA Modules:
  0.0 35.2 jit_solution(882447192993742769)
XLA Ops:
  0.6 30.2 %shard_map.85 = (f32[1024,128]{1,0:T(8,128)}, f32[512,128]{1,0:T(8,128)}, f32[1,1]{1,0:T(1,128)}) custom-call(bf16[1024,128]{1,0:T(8,128)(2,1)} %bitcast.7, bf16[256,128]{1,0:T(8,128)(2,1)} %bitcast.9, bf16[256,128]{1,0:T(8,128)(2,1)} %bitcast.10, bf16[4,128,128]{2,1,0:T(8,128)(2,1)} %fq_hbm.1, bf16[4,128,128]{2,1,0:T(8,128)(2,1)} %fk_hbm.1, s32[8]{0:T(128)} %samples.1), custom_call_target="tpu_custom_call" | custom-call | tf_op jit(solution)/shard_map/pallas_call | solution.py:281
  30.9 0.0 copy-start
  30.9 1.8 %convert_element_type.6 = bf16[1024,128]{1,0:T(8,128)(2,1)} convert(f32[1024,128]{1,0:T(8,128)} %get-tuple-element.6) | non-fusion elementwise | flops 131072 | bytes 786432 | tf_op jit(solution)/shard_map/convert_element_type | solution.py:318
  32.7 0.0 copy-done
  32.7 0.7 %copy.11 = f32[1,128,4,128]{3,2,1,0:T(4,128)} copy(f32[1,128,4,128]{3,2,1,0:T(4,128)S(1)} %bitcast.8) | data formatting | bytes 524288
Async XLA Ops:
  30.9 1.8 %copy-start = (f32[512,128]{1,0:T(8,128)S(1)}, f32[512,128]{1,0:T(8,128)}, u32[]{:S(2)}) copy-start(f32[512,128]{1,0:T(8,128)} %get-tuple-element.7) | copy-start | bytes 786436

commit v3 on v2

--- a/solution.py
+++ b/solution.py
@@ -22,12 +22,12 @@
     down = jnp.exp(jnp.min(logits, axis=axis, keepdims=True) - logits)
     up = up * (1.0 / jnp.sum(up, axis=axis, keepdims=True))
     down = down * (1.0 / jnp.sum(down, axis=axis, keepdims=True))
-    return jnp.concatenate([up, down], axis=axis).astype(jnp.bfloat16)
+    return jnp.concatenate([up, down], axis=axis)
 
 
 def kernel(
-    n, nh, q_hbm, k_hbm, v_hbm, fq_hbm, fk_hbm, samples, out32, teacher, loss,
-    kv, q_raw, fq, fk, fk_t, rows32, qs_t, phi_q, state, num, den, top, tot, acc, column, below, plane, total,
+    n, nh, q_hbm, k_hbm, v_hbm, fq_hbm, fk_hbm, samples_hbm, student, teacher, loss,
+    samples, kv, q_raw, fq, fk, fk_t, rows32, qs_t, phi_q, phi_s, state, num, den, num_s, den_s, top, tot, acc, out32, column, below, plane, total,
     local_sem, recv_sem, send_sem, up_sem, plane_send, plane_recv, down_send, down_recv,
 ):
     tok, width = k_hbm.shape
@@ -41,7 +41,8 @@
     local = [
         pltpu.make_async_copy(src, dst, local_sem.at[i])
         for i, (src, dst) in enumerate(
-            [(q_hbm, q_raw), (fq_hbm, fq), (fk_hbm, fk), (k_hbm, kv.at[s, 0]), (v_hbm, kv.at[s, 1])]
+            [(q_hbm, q_raw), (fq_hbm, fq), (fk_hbm, fk), (k_hbm, kv.at[s, 0]), (v_hbm, kv.at[s, 1]),
+             (samples_hbm, samples)]
         )
     ]
     for copy in local:
@@ -83,7 +84,6 @@
         for j in range(2):
             hop(own[j], s, j, 1, partner).start()
 
-    pick = samples[s]
 
     def chosen(rows):
         block = rows[:BLOCK]
@@ -93,7 +93,7 @@
 
     def key_features(keys, h):
         logits = lax.dot_general(fk_t[h * 128:(h + 1) * 128, :], keys, NT, preferred_element_type=jnp.float32)
-        return soft_pair(logits, 0)
+        return soft_pair(logits, 0).astype(jnp.bfloat16)
 
     def weigh(keys, live):
         out = []
@@ -151,12 +151,15 @@
     state[...] = jnp.zeros_like(state)
     for copy in local:
         copy.wait()
+    pick = samples[s]
     rows32[...] = q_raw[...].astype(jnp.float32)
     for h in range(heads):
         mine = rows32[pl.ds(h, tok, stride=heads), :]
         qs_t[:, h * BLOCK:(h + 1) * BLOCK] = chosen(mine).T.astype(jnp.bfloat16)
         fk_t[h * 128:(h + 1) * 128, :] = fk[h].astype(jnp.float32).T.astype(jnp.bfloat16)
-        phi_q[h] = soft_pair(dot(mine.astype(jnp.bfloat16), fq[h]), 1)
+        phi = soft_pair(dot(mine.astype(jnp.bfloat16), fq[h]), 1)
+        phi_q[h] = phi.astype(jnp.bfloat16)
+        phi_s[h] = chosen(phi).astype(jnp.bfloat16)
 
     @pl.when(outer > 0)
     def _():
@@ -166,11 +169,18 @@
     place = lax.broadcasted_iota(jnp.int32, (tok, 2 * BLOCK), 0)
     row = lax.broadcasted_iota(jnp.int32, (tok, 2 * BLOCK), 1) % BLOCK + pick * BLOCK
     mix(weigh(keys, place <= row), values)
+
+    @pl.when(outer > 1)
+    def _():
+        relay(s - 4)
+
     causal = lax.broadcasted_iota(jnp.int32, (tok, tok), 0) >= lax.broadcasted_iota(jnp.int32, (tok, tok), 1)
     for h in range(heads):
         inner = jnp.where(causal, dot(phi_q[h], key_features(keys, h)), 0.0)
         num[h] = dot(inner.astype(jnp.bfloat16), values)
         den[h] = jnp.broadcast_to(jnp.sum(inner, axis=1, keepdims=True), (tok, width))
+        num_s[h] = chosen(num[h])
+        den_s[h] = chosen(den[h])
 
     @pl.when(y == 1)
     def _():
@@ -179,25 +189,26 @@
     def lap(d, carry):
         absorb(s - 2 * d, False)
 
-        @pl.when(d < outer)
+        @pl.when(d + 2 <= outer)
         def _():
-            relay(s - 2 * d - 2)
+            relay(s - 2 * d - 4)
 
         absorb(partner - 2 * d, True)
         return carry
 
     lax.fori_loop(1, outer + 1, lap, 0)
+
+    def finish(h, phi, numer, denom):
+        inter = dot(phi[h], state[h].astype(jnp.bfloat16))
+        result = (numer[h] + inter[:, :width]) / (denom[h] + inter[:, width:])
+        return result.astype(jnp.bfloat16).astype(jnp.float32)
 
     part = jnp.zeros((8, width), jnp.float32)
     for h in range(heads):
         cols = slice(h * BLOCK, (h + 1) * BLOCK)
-        inter = dot(phi_q[h], state[h].astype(jnp.bfloat16))
-        result = (num[h] + inter[:, :width]) / (den[h] + inter[:, width:])
-        result = result.astype(jnp.bfloat16).astype(jnp.float32)
-        out32[pl.ds(h, tok, stride=heads), :] = result
         mixed = (acc[:, cols] / tot[:, cols]).T
         teacher[pl.ds(h, BLOCK, stride=heads), :] = mixed
-        gap = chosen(result) - mixed
+        gap = finish(h, phi_s, num_s, den_s) - mixed
         part = part + jnp.sum((gap * gap).reshape(BLOCK // 8, 8, width), axis=0)
 
     def send(src, dst, send_sem, recv_sem, device):
@@ -230,12 +241,20 @@
         plane[mate] = column[...]
         for copy in across:
             copy.start()
+
+    for h in range(heads):
+        out32[pl.ds(h, tok, stride=heads), :] = finish(h, phi_q, num, den)
+
+    @pl.when(outer == last)
+    def _():
         for copy in across:
             copy.wait()
         total[...] = jnp.sum(plane[...], axis=0)
         for copy in downward:
             copy.start()
 
+    student[...] = out32[...].astype(jnp.bfloat16)
+
     @pl.when(outer < last)
     def _():
         for j in range(2):
@@ -274,20 +293,21 @@
 def on_device(n, nh, queries, keys, values, feat_q, feat_k, samples):
     tok, heads, width = queries.shape
     bf16, f32 = jnp.bfloat16, jnp.float32
-    anywhere = pl.BlockSpec(memory_space=pl.ANY)
+    in_hbm = pl.BlockSpec(memory_space=pltpu.HBM)
     in_vmem = pl.BlockSpec(memory_space=pltpu.VMEM)
     in_smem = pl.BlockSpec(memory_space=pltpu.SMEM)
     dma = pltpu.SemaphoreType.DMA
     student, teacher, loss = pl.pallas_call(
         functools.partial(kernel, n, nh),
         out_shape=(
-            jax.ShapeDtypeStruct((tok * heads, width), f32),
+            jax.ShapeDtypeStruct((tok * heads, width), bf16),
             jax.ShapeDtypeStruct((BLOCK * heads, width), f32),
             jax.ShapeDtypeStruct((1, 1), f32),
         ),
-        in_specs=[anywhere] * 5 + [in_smem],
+        in_specs=[in_hbm] * 6,
         out_specs=(in_vmem, in_vmem, in_smem),
         scratch_shapes=[
+            pltpu.SMEM((n,), jnp.int32),
             pltpu.VMEM((n, 2, tok, width), bf16),
             pltpu.VMEM((tok * heads, width), bf16),
             pltpu.VMEM(feat_q.shape, bf16),
@@ -296,26 +316,31 @@
             pltpu.VMEM((tok * heads, width), f32),
             pltpu.VMEM((width, heads * BLOCK), bf16),
             pltpu.VMEM((heads, tok, 256), bf16),
+            pltpu.VMEM((heads, BLOCK, 256), bf16),
             pltpu.VMEM((heads, 256, 2 * width), f32),
             pltpu.VMEM((heads, tok, width), f32),
             pltpu.VMEM((heads, tok, width), f32),
+            pltpu.VMEM((heads, BLOCK, width), f32),
+            pltpu.VMEM((heads, BLOCK, width), f32),
             pltpu.VMEM((1, heads * BLOCK), f32),
             pltpu.VMEM((1, heads * BLOCK), f32),
             pltpu.VMEM((width, heads * BLOCK), f32),
+            pltpu.VMEM((tok * heads, width), f32),
             pltpu.VMEM((8, width), f32),
             pltpu.VMEM((8, width), f32),
             pltpu.VMEM((2 * nh, 8, width), f32),
             pltpu.VMEM((8, width), f32),
-            dma((5,)), dma((n, 2)), dma((2, n, 2)), dma((2,)), dma((2 * nh,)), dma((2 * nh,)), dma((n // 2,)), dma((1,)),
+            dma((6,)), dma((n, 2)), dma((2, n, 2)), dma((2,)), dma((2 * nh,)), dma((2 * nh,)), dma((n // 2,)), dma((1,)),
         ],
         compiler_params=pltpu.CompilerParams(
-            collective_id=0, has_side_effects=True, vmem_limit_bytes=60 * 1024 * 1024
+            collective_id=0, has_side_effects=True, vmem_limit_bytes=24 * 1024 * 1024
         ),
-    )(
-        queries.reshape(tok * heads, width), keys.reshape(tok, width), values.reshape(tok, width),
-        feat_q, feat_k, samples,
-    )
-    return student.reshape(tok, heads, width).astype(bf16), teacher.reshape(1, BLOCK, heads, width), loss.reshape(())
+    )(*(
+        pltpu.with_memory_space_constraint(x, pltpu.HBM) for x in (
+            queries.reshape(tok * heads, width), keys.reshape(tok, width), values.reshape(tok, width), feat_q, feat_k, samples,
+        )
+    ))
+    return student.reshape(tok, heads, width), teacher.reshape(1, BLOCK, heads, width), loss.reshape(())
 
 
 def solution(mesh):

time: 35.3 us -> 33.9 us (0.960)
  other arithmetic: 1.81 us -> 0 us
  local copies, waits for them, and re-layouts: 0.71 us -> 1.41 us
    convert_element_type x1 -> x0, other arithmetic: 1.81 us -> none  [on_device(): student.reshape(tok, heads, width).astype(bf16)]
    unnamed x3 -> x2, local copies, waits for them, and re-layouts: 0.71 us -> 1.41 us
where the time goes in v3:
time: 33.9 us; the launch traced here: 33.8 us
  Pallas kernels  30 us (88%)
  between operations  2.33 us (7%)
  local copies, waits for them, and re-layouts  1.41 us (4%)
    pallas_call x1, Pallas kernels, on_device(): pl.pallas_call(functools.partial(kernel, n, nh), out_shape=(jax.ShapeDtyp...  30 us
    unnamed x2, local copies, waits for them, and re-layouts  1.41 us

profile of v3, /device:TPU:0, one launch (start us, length us, event | category | flops | bytes accessed | tf_op | source)
XLA Modules:
  0.0 33.8 jit_solution(15032483338372150825)
XLA Ops:
  0.6 30.0 %shard_map.85 = (bf16[1024,128]{1,0:T(8,128)(2,1)S(1)}, f32[512,128]{1,0:T(8,128)S(1)}, f32[1,1]{1,0:T(1,128)}) custom-call(bf16[1024,128]{1,0:T(8,128)(2,1)} %bitcast.8, bf16[256,128]{1,0:T(8,128)(2,1)} %bitcast.9, bf16[256,128]{1,0:T(8,128)(2,1)} %bitcast.10, bf16[4,128,128]{2,1,0:T(8,128)(2,1)} %fq_hbm.1, bf16[4,128,128]{2,1,0:T(8,128)(2,1)} %fk_hbm.1, ...), custom_call_target="tpu_custom_call" | custom-call | tf_op jit(solution)/shard_map/pallas_call | solution.py:300
  30.7 0.7 %copy.12 = bf16[256,4,128]{2,1,0:T(4,128)(2,1)} copy(bf16[256,4,128]{2,1,0:T(4,128)(2,1)S(1)} %bitcast.7) | data formatting | bytes 524288
  31.4 0.7 %copy.13 = f32[1,128,4,128]{3,2,1,0:T(4,128)} copy(f32[1,128,4,128]{3,2,1,0:T(4,128)S(1)} %bitcast.6) | data formatting | bytes 524288

commit v4 on v3

--- a/solution.py
+++ b/solution.py
@@ -18,8 +18,9 @@
 
 
 def soft_pair(logits, axis):
-    up = jnp.exp(logits - jnp.max(logits, axis=axis, keepdims=True))
-    down = jnp.exp(jnp.min(logits, axis=axis, keepdims=True) - logits)
+    logits = logits * LOG2E
+    up = jnp.exp2(logits - jnp.max(logits, axis=axis, keepdims=True))
+    down = jnp.exp2(jnp.min(logits, axis=axis, keepdims=True) - logits)
     up = up * (1.0 / jnp.sum(up, axis=axis, keepdims=True))
     down = down * (1.0 / jnp.sum(down, axis=axis, keepdims=True))
     return jnp.concatenate([up, down], axis=axis)
@@ -27,7 +28,7 @@
 
 def kernel(
     n, nh, q_hbm, k_hbm, v_hbm, fq_hbm, fk_hbm, samples_hbm, student, teacher, loss,
-    samples, kv, q_raw, fq, fk, fk_t, rows32, qs_t, phi_q, phi_s, state, num, den, num_s, den_s, top, tot, acc, out32, column, below, plane, total,
+    samples, kv, q_raw, fq, fk, fk_t, rows32, qs_t, phi_q, phi_s, feats, state, state_low, num, den, num_s, den_s, top, tot, acc, out32, column, below, plane, total,
     local_sem, recv_sem, send_sem, up_sem, plane_send, plane_recv, down_send, down_recv,
 ):
     tok, width = k_hbm.shape
@@ -91,9 +92,10 @@
             block = jnp.where(pick == b, rows[b * BLOCK:(b + 1) * BLOCK], block)
         return block
 
-    def key_features(keys, h):
-        logits = lax.dot_general(fk_t[h * 128:(h + 1) * 128, :], keys, NT, preferred_element_type=jnp.float32)
-        return soft_pair(logits, 0).astype(jnp.bfloat16)
+    def key_features(keys):
+        logits = lax.dot_general(fk_t[...], keys, NT, preferred_element_type=jnp.float32)
+        for h in range(heads):
+            feats[h * 256:(h + 1) * 256, :] = soft_pair(logits[h * 128:(h + 1) * 128], 0).astype(jnp.bfloat16)
 
     def weigh(keys, live):
         out = []
@@ -129,14 +131,13 @@
             arrived(slot, 0)
         keys = kv[slot, 0]
         weighed = weigh(keys, None)
-        features = [key_features(keys, h) for h in range(heads)]
+        key_features(keys)
         if wait:
             arrived(slot, 1)
         values = kv[slot, 1]
         mix(weighed, values)
         values_wide = jnp.concatenate([values, jnp.ones_like(values)], axis=1)
-        for h in range(heads):
-            state[h] += dot(features[h], values_wide)
+        state[...] += dot(feats[...], values_wide)
 
     def relay(slot):
         for j in range(2):
@@ -175,8 +176,9 @@
         relay(s - 4)
 
     causal = lax.broadcasted_iota(jnp.int32, (tok, tok), 0) >= lax.broadcasted_iota(jnp.int32, (tok, tok), 1)
+    key_features(keys)
     for h in range(heads):
-        inner = jnp.where(causal, dot(phi_q[h], key_features(keys, h)), 0.0)
+        inner = jnp.where(causal, dot(phi_q[h], feats[h * 256:(h + 1) * 256, :]), 0.0)
         num[h] = dot(inner.astype(jnp.bfloat16), values)
         den[h] = jnp.broadcast_to(jnp.sum(inner, axis=1, keepdims=True), (tok, width))
         num_s[h] = chosen(num[h])
@@ -199,10 +201,11 @@
     lax.fori_loop(1, outer + 1, lap, 0)
 
     def finish(h, phi, numer, denom):
-        inter = dot(phi[h], state[h].astype(jnp.bfloat16))
+        inter = dot(phi[h], state_low[h * 256:(h + 1) * 256, :])
         result = (numer[h] + inter[:, :width]) / (denom[h] + inter[:, width:])
         return result.astype(jnp.bfloat16).astype(jnp.float32)
 
+    state_low[...] = state[...].astype(jnp.bfloat16)
     part = jnp.zeros((8, width), jnp.float32)
     for h in range(heads):
         cols = slice(h * BLOCK, (h + 1) * BLOCK)
@@ -317,7 +320,9 @@
             pltpu.VMEM((width, heads * BLOCK), bf16),
             pltpu.VMEM((heads, tok, 256), bf16),
             pltpu.VMEM((heads, BLOCK, 256), bf16),
-            pltpu.VMEM((heads, 256, 2 * width), f32),
+            pltpu.VMEM((heads * 256, tok), bf16),
+            pltpu.VMEM((heads * 256, 2 * width), f32),
+            pltpu.VMEM((heads * 256, 2 * width), bf16),
             pltpu.VMEM((heads, tok, width), f32),
             pltpu.VMEM((heads, tok, width), f32),
             pltpu.VMEM((heads, BLOCK, width), f32),

time: 33.9 us -> 34.1 us (level)
  no operation moved by 1% of the time
where the time goes in v4:
time: 34.1 us; the launch traced here: 33.9 us
  Pallas kernels  30.2 us (89%)
  between operations  2.33 us (7%)
  local copies, waits for them, and re-layouts  1.41 us (4%)
    pallas_call x1, Pallas kernels, on_device(): pl.pallas_call(functools.partial(kernel, n, nh), out_shape=(jax.ShapeDtyp...  30.2 us
    unnamed x2, local copies, waits for them, and re-layouts  1.41 us

profile of v4, /device:TPU:0, one launch (start us, length us, event | category | flops | bytes accessed | tf_op | source)
XLA Modules:
  0.0 33.9 jit_solution(9379746737707740413)
XLA Ops:
  0.6 30.2 %shard_map.85 = (bf16[1024,128]{1,0:T(8,128)(2,1)S(1)}, f32[512,128]{1,0:T(8,128)S(1)}, f32[1,1]{1,0:T(1,128)}) custom-call(bf16[1024,128]{1,0:T(8,128)(2,1)} %bitcast.8, bf16[256,128]{1,0:T(8,128)(2,1)} %bitcast.9, bf16[256,128]{1,0:T(8,128)(2,1)} %bitcast.10, bf16[4,128,128]{2,1,0:T(8,128)(2,1)} %fq_hbm.1, bf16[4,128,128]{2,1,0:T(8,128)(2,1)} %fk_hbm.1, ...), custom_call_target="tpu_custom_call" | custom-call | tf_op jit(solution)/shard_map/pallas_call | solution.py:303
  30.8 0.7 %copy.12 = bf16[256,4,128]{2,1,0:T(4,128)(2,1)} copy(bf16[256,4,128]{2,1,0:T(4,128)(2,1)S(1)} %bitcast.7) | data formatting | bytes 524288
  31.5 0.7 %copy.13 = f32[1,128,4,128]{3,2,1,0:T(4,128)} copy(f32[1,128,4,128]{3,2,1,0:T(4,128)S(1)} %bitcast.6) | data formatting | bytes 524288

commit v5 on v4

--- a/solution.py
+++ b/solution.py
@@ -139,8 +139,10 @@
         values_wide = jnp.concatenate([values, jnp.ones_like(values)], axis=1)
         state[...] += dot(feats[...], values_wide)
 
-    def relay(slot):
-        for j in range(2):
+    def relay(d, j):
+        @pl.when(d <= outer)
+        def _():
+            slot = s - 2 * d
             arrived(slot, j)
 
             @pl.when(outer < last)
@@ -155,25 +157,25 @@
     pick = samples[s]
     rows32[...] = q_raw[...].astype(jnp.float32)
     for h in range(heads):
+        qs_t[:, h * BLOCK:(h + 1) * BLOCK] = chosen(rows32[pl.ds(h, tok, stride=heads), :]).T.astype(jnp.bfloat16)
+        fk_t[h * 128:(h + 1) * 128, :] = fk[h].astype(jnp.float32).T.astype(jnp.bfloat16)
+
+    relay(1, 0)
+    for h in range(heads):
         mine = rows32[pl.ds(h, tok, stride=heads), :]
-        qs_t[:, h * BLOCK:(h + 1) * BLOCK] = chosen(mine).T.astype(jnp.bfloat16)
-        fk_t[h * 128:(h + 1) * 128, :] = fk[h].astype(jnp.float32).T.astype(jnp.bfloat16)
         phi = soft_pair(dot(mine.astype(jnp.bfloat16), fq[h]), 1)
         phi_q[h] = phi.astype(jnp.bfloat16)
         phi_s[h] = chosen(phi).astype(jnp.bfloat16)
-
-    @pl.when(outer > 0)
-    def _():
-        relay(s - 2)
+        if h == heads // 2 - 1:
+            relay(1, 1)
+    relay(2, 0)
 
     keys, values = kv[s, 0], kv[s, 1]
     place = lax.broadcasted_iota(jnp.int32, (tok, 2 * BLOCK), 0)
     row = lax.broadcasted_iota(jnp.int32, (tok, 2 * BLOCK), 1) % BLOCK + pick * BLOCK
     mix(weigh(keys, place <= row), values)
 
-    @pl.when(outer > 1)
-    def _():
-        relay(s - 4)
+    relay(2, 1)
 
     causal = lax.broadcasted_iota(jnp.int32, (tok, tok), 0) >= lax.broadcasted_iota(jnp.int32, (tok, tok), 1)
     key_features(keys)
@@ -191,11 +193,9 @@
     def lap(d, carry):
         absorb(s - 2 * d, False)
 
-        @pl.when(d + 2 <= outer)
-        def _():
-            relay(s - 2 * d - 4)
-
+        relay(d + 2, 0)
         absorb(partner - 2 * d, True)
+        relay(d + 2, 1)
         return carry
 
     lax.fori_loop(1, outer + 1, lap, 0)
@@ -245,9 +245,6 @@
         for copy in across:
             copy.start()
 
-    for h in range(heads):
-        out32[pl.ds(h, tok, stride=heads), :] = finish(h, phi_q, num, den)
-
     @pl.when(outer == last)
     def _():
         for copy in across:
@@ -256,6 +253,8 @@
         for copy in downward:
             copy.start()
 
+    for h in range(heads):
+        out32[pl.ds(h, tok, stride=heads), :] = finish(h, phi_q, num, den)
     student[...] = out32[...].astype(jnp.bfloat16)
 
     @pl.when(outer < last)

time: 34.1 us -> 34.1 us (level)
  no operation moved by 1% of the time
where the time goes in v5:
time: 34.1 us; the launch traced here: 33.9 us
  Pallas kernels  30.2 us (89%)
  between operations  2.33 us (7%)
  local copies, waits for them, and re-layouts  1.41 us (4%)
    pallas_call x1, Pallas kernels, on_device(): pl.pallas_call(functools.partial(kernel, n, nh), out_shape=(jax.ShapeDtyp...  30.2 us
    unnamed x2, local copies, waits for them, and re-layouts  1.41 us

profile of v5, /device:TPU:0, one launch (start us, length us, event | category | flops | bytes accessed | tf_op | source)
XLA Modules:
  0.0 33.9 jit_solution(4099288812677844525)
XLA Ops:
  0.6 30.2 %shard_map.85 = (bf16[1024,128]{1,0:T(8,128)(2,1)S(1)}, f32[512,128]{1,0:T(8,128)S(1)}, f32[1,1]{1,0:T(1,128)}) custom-call(bf16[1024,128]{1,0:T(8,128)(2,1)} %bitcast.8, bf16[256,128]{1,0:T(8,128)(2,1)} %bitcast.9, bf16[256,128]{1,0:T(8,128)(2,1)} %bitcast.10, bf16[4,128,128]{2,1,0:T(8,128)(2,1)} %fq_hbm.1, bf16[4,128,128]{2,1,0:T(8,128)(2,1)} %fk_hbm.1, ...), custom_call_target="tpu_custom_call" | custom-call | tf_op jit(solution)/shard_map/pallas_call | solution.py:302
  30.8 0.7 %copy.12 = bf16[256,4,128]{2,1,0:T(4,128)(2,1)} copy(bf16[256,4,128]{2,1,0:T(4,128)(2,1)S(1)} %bitcast.7) | data formatting | bytes 524288
  31.5 0.7 %copy.13 = f32[1,128,4,128]{3,2,1,0:T(4,128)} copy(f32[1,128,4,128]{3,2,1,0:T(4,128)S(1)} %bitcast.6) | data formatting | bytes 524288

commit v6 on v5

--- a/solution.py
+++ b/solution.py
@@ -140,7 +140,7 @@
         state[...] += dot(feats[...], values_wide)
 
     def relay(d, j):
-        @pl.when(d <= outer)
+        @pl.when(outer >= d)
         def _():
             slot = s - 2 * d
             arrived(slot, j)
@@ -149,7 +149,12 @@
             def _():
                 hop(kv.at[slot, j], slot, j, 0, s + 2).start()
 
-            hop(kv.at[slot, j], slot, j, 1, partner).start()
+            if isinstance(d, int) and (d, j) == (1, 1):
+                @pl.when(y + last - outer > 0)
+                def _():
+                    hop(kv.at[slot, j], slot, j, 1, partner).start()
+            else:
+                hop(kv.at[slot, j], slot, j, 1, partner).start()
 
     state[...] = jnp.zeros_like(state)
     for copy in local:
@@ -190,11 +195,23 @@
     def _():
         absorb(partner, True)
 
+        @pl.when(outer == last - 1)
+        def _():
+            hop(kv.at[partner, 1], partner, 1, 0, s + 2).start()
+
     def lap(d, carry):
         absorb(s - 2 * d, False)
 
         relay(d + 2, 0)
-        absorb(partner - 2 * d, True)
+
+        @pl.when(d == outer)
+        def _():
+            absorb(partner - 2, True)
+
+        @pl.when(d > 1)
+        def _():
+            absorb(partner - 2 * d, True)
+
         relay(d + 2, 1)
         return carry
 
@@ -267,6 +284,10 @@
         for j in range(2):
             hop(own[j], s, j, 1, partner).wait_send()
 
+    @pl.when(s == 2 * last - 1)
+    def _():
+        hop(kv.at[partner, 1], partner, 1, 0, s + 2).wait_send()
+
     def drain(d, carry):
         near = s - 2 * d
         for j in range(2):
@@ -274,7 +295,11 @@
             def _():
                 hop(kv.at[near, j], near, j, 0, s + 2).wait_send()
 
-            hop(kv.at[near, j], near, j, 1, partner).wait_send()
+        hop(kv.at[near, 0], near, 0, 1, partner).wait_send()
+
+        @pl.when(y + last - outer + d > 1)
+        def _():
+            hop(kv.at[near, 1], near, 1, 1, partner).wait_send()
         return carry
 
     lax.fori_loop(1, outer + 1, drain, 0)

time: 34.1 us -> 34.1 us (level)
  no operation moved by 1% of the time
where the time goes in v6:
time: 34.1 us; the launch traced here: 33.9 us
  Pallas kernels  30.2 us (89%)
  between operations  2.33 us (7%)
  local copies, waits for them, and re-layouts  1.41 us (4%)
    pallas_call x1, Pallas kernels, on_device(): pl.pallas_call(functools.partial(kernel, n, nh), out_shape=(jax.ShapeDtyp...  30.2 us
    unnamed x2, local copies, waits for them, and re-layouts  1.41 us

profile of v6, /device:TPU:0, one launch (start us, length us, event | category | flops | bytes accessed | tf_op | source)
XLA Modules:
  0.0 33.9 jit_solution(10723178462327202211)
XLA Ops:
  0.6 30.2 %shard_map.85 = (bf16[1024,128]{1,0:T(8,128)(2,1)S(1)}, f32[512,128]{1,0:T(8,128)S(1)}, f32[1,1]{1,0:T(1,128)}) custom-call(bf16[1024,128]{1,0:T(8,128)(2,1)} %bitcast.8, bf16[256,128]{1,0:T(8,128)(2,1)} %bitcast.9, bf16[256,128]{1,0:T(8,128)(2,1)} %bitcast.10, bf16[4,128,128]{2,1,0:T(8,128)(2,1)} %fq_hbm.1, bf16[4,128,128]{2,1,0:T(8,128)(2,1)} %fk_hbm.1, ...), custom_call_target="tpu_custom_call" | custom-call | tf_op jit(solution)/shard_map/pallas_call | solution.py:327
  30.8 0.7 %copy.12 = bf16[256,4,128]{2,1,0:T(4,128)(2,1)} copy(bf16[256,4,128]{2,1,0:T(4,128)(2,1)S(1)} %bitcast.7) | data formatting | bytes 524288
  31.5 0.7 %copy.13 = f32[1,128,4,128]{3,2,1,0:T(4,128)} copy(f32[1,128,4,128]{3,2,1,0:T(4,128)S(1)} %bitcast.6) | data formatting | bytes 524288

commit v7 on v6

--- a/solution.py
+++ b/solution.py
@@ -37,13 +37,14 @@
     outer, y = s // 2, s % 2
     last = n // 2 - 1
     partner = s + 1 - 2 * y
-    own = (k_hbm, v_hbm)
+    half = tok // 2
+    own = [x.at[i * half:(i + 1) * half, :] for x in (k_hbm, v_hbm) for i in range(2)]
 
     local = [
         pltpu.make_async_copy(src, dst, local_sem.at[i])
         for i, (src, dst) in enumerate(
-            [(q_hbm, q_raw), (fq_hbm, fq), (fk_hbm, fk), (k_hbm, kv.at[s, 0]), (v_hbm, kv.at[s, 1]),
-             (samples_hbm, samples)]
+            [(q_hbm, q_raw), (fq_hbm, fq), (fk_hbm, fk), (samples_hbm, samples)]
+            + [(own[p], kv.at[s, p]) for p in range(4)]
         )
     ]
     for copy in local:
@@ -77,12 +78,12 @@
 
     @pl.when(outer < last)
     def _():
-        for j in range(2):
+        for j in range(4):
             hop(own[j], s, j, 0, s + 2).start()
 
     @pl.when(y == 0)
     def _():
-        for j in range(2):
+        for j in range(4):
             hop(own[j], s, j, 1, partner).start()
 
 
@@ -124,37 +125,45 @@
             acc[:, cols] = mixed if fade is None else mixed + acc[:, cols] * fade
 
     def arrived(slot, j):
-        hop(kv.at[slot, j], slot, j, 0, partner).wait_recv()
+        for p in (2 * j, 2 * j + 1):
+            hop(kv.at[slot, p], slot, p, 0, partner).wait_recv()
+
+    def rows(slot, j):
+        return kv[slot, 2 * j:2 * j + 2].reshape(tok, width)
 
     def absorb(slot, wait):
         if wait:
             arrived(slot, 0)
-        keys = kv[slot, 0]
+        keys = rows(slot, 0)
         weighed = weigh(keys, None)
         key_features(keys)
         if wait:
             arrived(slot, 1)
-        values = kv[slot, 1]
+        values = rows(slot, 1)
         mix(weighed, values)
         values_wide = jnp.concatenate([values, jnp.ones_like(values)], axis=1)
         state[...] += dot(feats[...], values_wide)
 
     def relay(d, j):
-        @pl.when(outer >= d)
-        def _():
+        def hand_on(p):
             slot = s - 2 * d
-            arrived(slot, j)
+            hop(kv.at[slot, p], slot, p, 0, partner).wait_recv()
 
             @pl.when(outer < last)
             def _():
-                hop(kv.at[slot, j], slot, j, 0, s + 2).start()
+                hop(kv.at[slot, p], slot, p, 0, s + 2).start()
 
             if isinstance(d, int) and (d, j) == (1, 1):
                 @pl.when(y + last - outer > 0)
                 def _():
-                    hop(kv.at[slot, j], slot, j, 1, partner).start()
+                    hop(kv.at[slot, p], slot, p, 1, partner).start()
             else:
-                hop(kv.at[slot, j], slot, j, 1, partner).start()
+                hop(kv.at[slot, p], slot, p, 1, partner).start()
+
+        @pl.when(outer >= d)
+        def _():
+            hand_on(2 * j)
+            hand_on(2 * j + 1)
 
     state[...] = jnp.zeros_like(state)
     for copy in local:
@@ -175,7 +184,7 @@
             relay(1, 1)
     relay(2, 0)
 
-    keys, values = kv[s, 0], kv[s, 1]
+    keys, values = rows(s, 0), rows(s, 1)
     place = lax.broadcasted_iota(jnp.int32, (tok, 2 * BLOCK), 0)
     row = lax.broadcasted_iota(jnp.int32, (tok, 2 * BLOCK), 1) % BLOCK + pick * BLOCK
     mix(weigh(keys, place <= row), values)
@@ -197,7 +206,8 @@
 
         @pl.when(outer == last - 1)
         def _():
-            hop(kv.at[partner, 1], partner, 1, 0, s + 2).start()
+            for p in (2, 3):
+                hop(kv.at[partner, p], partner, p, 0, s + 2).start()
 
     def lap(d, carry):
         absorb(s - 2 * d, False)
@@ -276,30 +286,33 @@
 
     @pl.when(outer < last)
     def _():
-        for j in range(2):
+        for j in range(4):
             hop(own[j], s, j, 0, s + 2).wait_send()
 
     @pl.when(y == 0)
     def _():
-        for j in range(2):
+        for j in range(4):
             hop(own[j], s, j, 1, partner).wait_send()
 
     @pl.when(s == 2 * last - 1)
     def _():
-        hop(kv.at[partner, 1], partner, 1, 0, s + 2).wait_send()
+        for p in (2, 3):
+            hop(kv.at[partner, p], partner, p, 0, s + 2).wait_send()
 
     def drain(d, carry):
         near = s - 2 * d
-        for j in range(2):
-            @pl.when(outer < last)
-            def _():
-                hop(kv.at[near, j], near, j, 0, s + 2).wait_send()
-
-        hop(kv.at[near, 0], near, 0, 1, partner).wait_send()
+        @pl.when(outer < last)
+        def _():
+            for p in range(4):
+                hop(kv.at[near, p], near, p, 0, s + 2).wait_send()
+
+        for p in range(2):
+            hop(kv.at[near, p], near, p, 1, partner).wait_send()
 
         @pl.when(y + last - outer + d > 1)
         def _():
-            hop(kv.at[near, 1], near, 1, 1, partner).wait_send()
+            for p in (2, 3):
+                hop(kv.at[near, p], near, p, 1, partner).wait_send()
         return carry
 
     lax.fori_loop(1, outer + 1, drain, 0)
@@ -335,7 +348,7 @@
         out_specs=(in_vmem, in_vmem, in_smem),
         scratch_shapes=[
             pltpu.SMEM((n,), jnp.int32),
-            pltpu.VMEM((n, 2, tok, width), bf16),
+            pltpu.VMEM((n, 4, tok // 2, width), bf16),
             pltpu.VMEM((tok * heads, width), bf16),
             pltpu.VMEM(feat_q.shape, bf16),
             pltpu.VMEM(feat_k.shape, bf16),
@@ -359,7 +372,7 @@
             pltpu.VMEM((8, width), f32),
             pltpu.VMEM((2 * nh, 8, width), f32),
             pltpu.VMEM((8, width), f32),
-            dma((6,)), dma((n, 2)), dma((2, n, 2)), dma((2,)), dma((2 * nh,)), dma((2 * nh,)), dma((n // 2,)), dma((1,)),
+            dma((8,)), dma((n, 4)), dma((2, n, 4)), dma((2,)), dma((2 * nh,)), dma((2 * nh,)), dma((n // 2,)), dma((1,)),
         ],
         compiler_params=pltpu.CompilerParams(
             collective_id=0, has_side_effects=True, vmem_limit_bytes=24 * 1024 * 1024

time: 34.1 us -> 34.1 us (level)
  no operation moved by 1% of the time
where the time goes in v7:
time: 34.1 us; the launch traced here: 33.9 us
  Pallas kernels  30.2 us (89%)
  between operations  2.33 us (7%)
  local copies, waits for them, and re-layouts  1.41 us (4%)
    pallas_call x1, Pallas kernels, on_device(): pl.pallas_call(functools.partial(kernel, n, nh), out_shape=(jax.ShapeDtyp...  30.2 us
    unnamed x2, local copies, waits for them, and re-layouts  1.41 us

profile of v7, /device:TPU:0, one launch (start us, length us, event | category | flops | bytes accessed | tf_op | source)
XLA Modules:
  0.0 33.9 jit_solution(10508591692465520627)
XLA Ops:
  0.6 30.2 %shard_map.85 = (bf16[1024,128]{1,0:T(8,128)(2,1)S(1)}, f32[512,128]{1,0:T(8,128)S(1)}, f32[1,1]{1,0:T(1,128)}) custom-call(bf16[1024,128]{1,0:T(8,128)(2,1)} %bitcast.8, bf16[256,128]{1,0:T(8,128)(2,1)} %bitcast.9, bf16[256,128]{1,0:T(8,128)(2,1)} %bitcast.10, bf16[4,128,128]{2,1,0:T(8,128)(2,1)} %fq_hbm.1, bf16[4,128,128]{2,1,0:T(8,128)(2,1)} %fk_hbm.1, ...), custom_call_target="tpu_custom_call" | custom-call | tf_op jit(solution)/shard_map/pallas_call | solution.py:340
  30.8 0.7 %copy.12 = bf16[256,4,128]{2,1,0:T(4,128)(2,1)} copy(bf16[256,4,128]{2,1,0:T(4,128)(2,1)S(1)} %bitcast.7) | data formatting | bytes 524288
  31.5 0.7 %copy.13 = f32[1,128,4,128]{3,2,1,0:T(4,128)} copy(f32[1,128,4,128]{3,2,1,0:T(4,128)S(1)} %bitcast.6) | data formatting | bytes 524288
